TPU v7x, 32 devices: a whole 2x2x4 slice. The times are simulated.
32 devices in a mesh: grp: 4 (over y, core), blk: 8 (over z, x).
Axes of the slice: x: 2, y: 2, z: 4, core: 2. Of those that a mesh axis runs over, the one named last changes fastest.
Arguments:
- ratings: bfloat16 [8, 32768, 512], P(None, ('grp', 'blk')), may hold values from -6 to 6
- rated: int32 [8, 32768, 512], P(None, ('grp', 'blk')), may hold values 0 or 1
- user_factors: float32 [32768, 256], P(('grp', 'blk')), may hold values from -1.5 to 1.5
- item_ahead: bfloat16 [8192, 256], P(('grp', 'blk')), may hold values from -1.5 to 1.5
- item_behind: bfloat16 [8192, 256], P(('grp', 'blk')), may hold values from -1.5 to 1.5
- owners: int32 [2, 32], replicated, may hold values from 0 to 31, each once within a row
Outputs:
- user_out: float32 [32768, 256], P(('grp', 'blk'))
- ahead_out: bfloat16 [8192, 256], P(('grp', 'blk'))
- behind_out: bfloat16 [8192, 256], P(('grp', 'blk'))
Inputs may be any that keep to these rules, and one draw needn't show every extreme that they name: `owners`: each row is a permutation of 0 .. 31.
All inputs are finite; a program needn't handle non-finite values. No bound on the sum of `rated` on one device may be relied on, other than what follows from the above.
Results may differ from a plain program's by a relative error of at most 0.0086.
Values may be sent and summed in bfloat16 or wider, within the bound.
A program may use at most 128 MiB of HBM per device.

v0:
```python
import jax
import jax.numpy as jnp
from jax import lax
from jax.sharding import PartitionSpec as P

RATE = 0.005
DECAY = 0.05


def from_behind(array, axis, by):
    count = lax.axis_size(axis)
    return lax.ppermute(array, axis, [(i, (i + by) % count) for i in range(count)])


def body(ratings, rated, user_factors, item_ahead, item_behind, owners):
    half = item_ahead.shape[0]
    users = user_factors
    ahead = item_ahead
    behind = item_behind
    strata = ratings.shape[0]
    for stratum in range(strata):
        if stratum == strata // 2:
            row_count = lax.axis_size("blk")
            group_count = lax.axis_size("grp")
            group_self = lax.axis_index("grp")
            column_self = lax.axis_index("blk")
            targets = jnp.arange(group_count, dtype=jnp.int32) * row_count + column_self
            pieces = (
                lax.all_gather(ahead, "blk", axis=0, tiled=True),
                lax.all_gather(behind, "blk", axis=0, tiled=True),
            )
            width = pieces[0].shape[0] // half
            source = group_self * row_count
            dest_a = lax.dynamic_slice_in_dim(owners[0], source, width)
            dest_b = lax.dynamic_slice_in_dim(owners[1], source, width)
            mask_a = (dest_a[:, None] == targets[None, :]).astype(jnp.bfloat16)
            mask_b = (dest_b[:, None] == targets[None, :]).astype(jnp.bfloat16)
            piece_a = pieces[0].reshape(width, half, -1)
            piece_b = pieces[1].reshape(width, half, -1)
            take_a = jnp.einsum("wg,whr->ghr", mask_a, piece_a, preferred_element_type=jnp.float32)
            take_b = jnp.einsum("wg,whr->ghr", mask_b, piece_b, preferred_element_type=jnp.float32)
            send_a = take_a.astype(jnp.bfloat16)
            send_b = take_b.astype(jnp.bfloat16)
            got_a, got_b = (
                lax.all_to_all(send_a, "grp", split_axis=0, concat_axis=0, tiled=True),
                lax.all_to_all(send_b, "grp", split_axis=0, concat_axis=0, tiled=True),
            )
            ahead = jnp.sum(got_a.astype(jnp.float32), 0).astype(jnp.bfloat16)
            behind = jnp.sum(got_b.astype(jnp.float32), 0).astype(jnp.bfloat16)
        block = jnp.concatenate([ahead, behind], axis=0)
        user_b = users.astype(jnp.bfloat16)
        pred = lax.dot_general(
            user_b, block, (((1,), (1,)), ((), ())), preferred_element_type=jnp.float32
        )
        err = jnp.where(
            rated[stratum] == 1, pred - ratings[stratum].astype(jnp.float32), 0.0
        ).astype(jnp.bfloat16)
        grad_user = jnp.dot(err, block, preferred_element_type=jnp.float32)
        grad_item = lax.dot_general(
            err, user_b, (((0,), (0,)), ((), ())), preferred_element_type=jnp.float32
        )
        users = users - RATE * (grad_user + DECAY * users)
        block_f = block.astype(jnp.float32)
        block = (block_f - RATE * (grad_item + DECAY * block_f)).astype(jnp.bfloat16)
        ahead = block[:half]
        behind = block[half:]
        if stratum < strata - 1:
            ahead = from_behind(ahead, ("grp", "blk"), 1)
            behind = from_behind(behind, ("grp", "blk"), -1)
    return (users, ahead, behind)


def solution(mesh):
    in_specs = (
        P(None, ("grp", "blk"), None),
        P(None, ("grp", "blk"), None),
        P(("grp", "blk"), None),
        P(("grp", "blk"), None),
        P(("grp", "blk"), None),
        P(),
    )
    out_specs = (P(("grp", "blk"), None), P(("grp", "blk"), None), P(("grp", "blk"), None))
    return jax.shard_map(body, mesh=mesh, in_specs=in_specs, out_specs=out_specs, check_vma=False)
```

profile of v0, /device:TPU:0, one launch (start us, length us, event | category | flops | bytes accessed | tf_op | source)
XLA Modules:
  0.0 230.9 jit_solution(17386755233823664467)
XLA Ops:
  7.2 11.5 %fusion.102 = (s32[1,1024,512]{2,1,0:T(8,128)}, s32[1,1024,512]{2,1,0:T(8,128)}, s32[1,1024,512]{2,1,0:T(8,128)}, s32[1,1024,512]{2,1,0:T(8,128)}, s32[1,1024,51...) fusion(s32[8,1024,512]{2,1,0:T(8,128)} %param.7), kind=kLoop, calls=%fused_computation.142 | loop fusion | bytes 33554432 | tf_op jit(solution)/shard_map/slice | solution.py:56
  20.5 5.9 %fusion.103 = (bf16[1,1024,512]{2,1,0:T(8,128)(2,1)}, bf16[1,1024,512]{2,1,0:T(8,128)(2,1)}, bf16[1,1024,512]{2,1,0:T(8,128)(2,1)}, bf16[1,1024,512]{2,1,0:T(8,1...) fusion(bf16[8,1024,512]{2,1,0:T(8,128)(2,1)} %param.6), kind=kLoop, calls=%fused_computation.143 | loop fusion | bytes 16777216 | tf_op jit(solution)/shard_map/slice | solution.py:56
  27.9 2.1 fusion.15
  31.1 2.9 %collective-permute-start = (bf16[256,256]{1,0:T(8,128)(2,1)}, bf16[256,256]{1,0:T(8,128)(2,1)S(1)}, u32[]{:S(2)}, u32[]{:S(2)}) collective-permute-start(bf16[256,256]{1,0:T(8,128)(2,1)} %get-tuple-element.34), channel_id=1, source_target_pairs={{0,1},{1,2},{2,3},{3,4},{4,5},{5,6},{6,7},{7,8},{8,9},{9,10},{10,1... | collective-permute-start | bytes 393224 | tf_op jit(solution)/shard_map/ppermute | solution.py:12
  34.1 3.4 %collective-permute-start.1 = (bf16[256,256]{1,0:T(8,128)(2,1)S(1)}, bf16[256,256]{1,0:T(8,128)(2,1)S(1)}, u32[]{:S(2)}, u32[]{:S(2)}) collective-permute-start(bf16[256,256]{1,0:T(8,128)(2,1)S(1)} %get-tuple-element.33), channel_id=1, source_target_pairs={{0,31},{1,0},{2,1},{3,2},{4,3},{5,4},{6,5},{7,6},{8,7},{9,8},{10,9... | collective-permute-start | bytes 393224 | tf_op jit(solution)/shard_map/ppermute | solution.py:12
  38.0 2.9 %copy.70 = s32[1,1024,512]{1,2,0:T(8,128)} copy(s32[1,1024,512]{2,1,0:T(8,128)} %get-tuple-element.9) | data formatting | bytes 4194304
  40.9 2.4 %copy.71 = bf16[1,1024,512]{1,2,0:T(8,128)(2,1)} copy(bf16[1,1024,512]{2,1,0:T(8,128)(2,1)} %get-tuple-element.17) | data formatting | bytes 2097152
  45.2 2.4 %copy.73 = bf16[1,1024,512]{1,2,0:T(8,128)(2,1)} copy(bf16[1,1024,512]{2,1,0:T(8,128)(2,1)} %get-tuple-element.16) | data formatting | bytes 2097152
  49.4 2.4 %copy.75 = bf16[1,1024,512]{1,2,0:T(8,128)(2,1)} copy(bf16[1,1024,512]{2,1,0:T(8,128)(2,1)} %get-tuple-element.15) | data formatting | bytes 2097152
  54.3 5.3 %collective-permute-start.3 = (bf16[256,256]{1,0:T(8,128)(2,1)S(1)}, bf16[256,256]{1,0:T(8,128)(2,1)S(1)}, u32[]{:S(2)}, u32[]{:S(2)}) collective-permute-start(bf16[256,256]{1,0:T(8,128)(2,1)S(1)} %get-tuple-element.31), channel_id=1, source_target_pairs={{0,31},{1,0},{2,1},{3,2},{4,3},{5,4},{6,5},{7,6},{8,7},{9,8},{10,9... | collective-permute-start | bytes 393224 | tf_op jit(solution)/shard_map/ppermute | solution.py:12
  60.1 3.5 %collective-permute-done.2 = bf16[256,256]{1,0:T(8,128)(2,1)S(1)} collective-permute-done((bf16[256,256]{1,0:T(8,128)(2,1)S(1)}, bf16[256,256]{1,0:T(8,128)(2,1)S(1)}, u32[]{:S(2)}, u32[]{:S(2)}) %collective-permute-start.2) | collective-permute-done | bytes 131104 | tf_op jit(solution)/shard_map/ppermute | solution.py:12
  64.7 5.3 %collective-permute-start.5 = (bf16[256,256]{1,0:T(8,128)(2,1)S(1)}, bf16[256,256]{1,0:T(8,128)(2,1)S(1)}, u32[]{:S(2)}, u32[]{:S(2)}) collective-permute-start(bf16[256,256]{1,0:T(8,128)(2,1)S(1)} %get-tuple-element.29), channel_id=1, source_target_pairs={{0,31},{1,0},{2,1},{3,2},{4,3},{5,4},{6,5},{7,6},{8,7},{9,8},{10,9... | collective-permute-start | bytes 393224 | tf_op jit(solution)/shard_map/ppermute | solution.py:12
  70.6 2.9 %collective-permute-done.4 = bf16[256,256]{1,0:T(8,128)(2,1)S(1)} collective-permute-done((bf16[256,256]{1,0:T(8,128)(2,1)S(1)}, bf16[256,256]{1,0:T(8,128)(2,1)S(1)}, u32[]{:S(2)}, u32[]{:S(2)}) %collective-permute-start.4) | collective-permute-done | bytes 131104 | tf_op jit(solution)/shard_map/ppermute | solution.py:12
  74.6 8.0 %collective-permute-done.6 = bf16[256,256]{1,0:T(8,128)(2,1)S(1)} collective-permute-done((bf16[256,256]{1,0:T(8,128)(2,1)S(1)}, bf16[256,256]{1,0:T(8,128)(2,1)S(1)}, u32[]{:S(2)}, u32[]{:S(2)}) %collective-permute-start.6) | collective-permute-done | bytes 131104 | tf_op jit(solution)/shard_map/ppermute | solution.py:12
  83.9 4.5 %collective-permute-done.7 = bf16[256,256]{1,0:T(8,128)(2,1)S(1)} collective-permute-done((bf16[256,256]{1,0:T(8,128)(2,1)S(1)}, bf16[256,256]{1,0:T(8,128)(2,1)S(1)}, u32[]{:S(2)}, u32[]{:S(2)}) %collective-permute-start.7) | collective-permute-done | bytes 131104 | tf_op jit(solution)/shard_map/ppermute | solution.py:12
  89.2 30.8 %all-gather.3.cloned.1.call-done = bf16[2048,256]{1,0:T(8,128)(2,1)} async-done(((bf16[256,256]{1,0:T(8,128)(2,1)}), bf16[2048,256]{1,0:T(8,128)(2,1)}) %all-gather.3.cloned.1.call-update) | async-done | bytes 1048592 | tf_op jit(solution)/shard_map/all_gather | solution.py:29
  120.0 2.0 convolution_convert_fusion.1
  122.9 3.5 %all-to-all-start = ((bf16[4,256,256]{2,1,0:T(8,128)(2,1)}), bf16[4,256,256]{2,1,0:T(8,128)(2,1)S(1)}, u32[]{:S(2)}, u32[]{:S(2)}) async-start(bf16[4,256,256]{2,1,0:T(8,128)(2,1)} %copy.47), calls=%async_computation | async-start | bytes 1048576 | tf_op jit(solution)/shard_map/all_to_all | solution.py:45
  126.4 35.2 %all-gather.5.cloned.1.call-done = bf16[2048,256]{1,0:T(8,128)(2,1)} async-done(((bf16[256,256]{1,0:T(8,128)(2,1)}), bf16[2048,256]{1,0:T(8,128)(2,1)}) %all-gather.5.cloned.1.call-update) | async-done | bytes 1048592 | tf_op jit(solution)/shard_map/all_gather | solution.py:30
  161.7 2.0 convolution_convert_fusion
  164.6 4.3 %all-to-all-start.1 = ((bf16[4,256,256]{2,1,0:T(8,128)(2,1)}), bf16[4,256,256]{2,1,0:T(8,128)(2,1)}, u32[]{:S(2)}, u32[]{:S(2)}) async-start(bf16[4,256,256]{2,1,0:T(8,128)(2,1)} %copy.49), calls=%async_computation.1 | async-start | bytes 1048576 | tf_op jit(solution)/shard_map/all_to_all | solution.py:46
  168.9 3.0 %copy.76 = s32[1,1024,512]{1,2,0:T(8,128)} copy(s32[1,1024,512]{2,1,0:T(8,128)} %get-tuple-element.6) | data formatting | bytes 4194304
  173.2 3.0 %copy.78 = s32[1,1024,512]{1,2,0:T(8,128)} copy(s32[1,1024,512]{2,1,0:T(8,128)} %get-tuple-element.5) | data formatting | bytes 4194304
  177.6 3.0 %copy.80 = s32[1,1024,512]{1,2,0:T(8,128)} copy(s32[1,1024,512]{2,1,0:T(8,128)} %get-tuple-element.4) | data formatting | bytes 4194304
  181.9 3.0 %copy.82 = s32[1,1024,512]{1,2,0:T(8,128)} copy(s32[1,1024,512]{2,1,0:T(8,128)} %get-tuple-element.3) | data formatting | bytes 4194304
  189.0 2.4 %fusion.7 = bf16[1024,512]{0,1:T(8,128)(2,1)S(1)} fusion(s32[1,1024,512]{1,2,0:T(8,128)} %copy.76, bf16[1,1024,512]{1,2,0:T(8,128)(2,1)} %copy.77, f32[1024,256]{1,0:T(8,128)S(1)} %fusion.25, bf16[256,256]{1,0:T(8,128)(2,1)S(1)} %reduce_sum.25, bf16[256,256]{1,0:T(8,128)(2,1)S(1)} %reduce_sum.24), kind=kOutput, calls=%fused_computation.11 | convolution fusion | flops 271843328 | bytes 5505024 | tf_op jit(solution)/shard_map/dot_general | solution.py:52
  192.5 4.8 %collective-permute-start.9 = (bf16[256,256]{1,0:T(8,128)(2,1)S(1)}, bf16[256,256]{1,0:T(8,128)(2,1)S(1)}, u32[]{:S(2)}, u32[]{:S(2)}) collective-permute-start(bf16[256,256]{1,0:T(8,128)(2,1)S(1)} %get-tuple-element.25), channel_id=1, source_target_pairs={{0,31},{1,0},{2,1},{3,2},{4,3},{5,4},{6,5},{7,6},{8,7},{9,8},{10,9... | collective-permute-start | bytes 393224 | tf_op jit(solution)/shard_map/ppermute | solution.py:12
  197.7 3.1 %collective-permute-done.8 = bf16[256,256]{1,0:T(8,128)(2,1)S(1)} collective-permute-done((bf16[256,256]{1,0:T(8,128)(2,1)S(1)}, bf16[256,256]{1,0:T(8,128)(2,1)S(1)}, u32[]{:S(2)}, u32[]{:S(2)}) %collective-permute-start.8) | collective-permute-done | bytes 131104 | tf_op jit(solution)/shard_map/ppermute | solution.py:12
  202.1 5.2 %collective-permute-start.11 = (bf16[256,256]{1,0:T(8,128)(2,1)S(1)}, bf16[256,256]{1,0:T(8,128)(2,1)S(1)}, u32[]{:S(2)}, u32[]{:S(2)}) collective-permute-start(bf16[256,256]{1,0:T(8,128)(2,1)S(1)} %get-tuple-element.23), channel_id=1, source_target_pairs={{0,31},{1,0},{2,1},{3,2},{4,3},{5,4},{6,5},{7,6},{8,7},{9,8},{10,9... | collective-permute-start | bytes 393224 | tf_op jit(solution)/shard_map/ppermute | solution.py:12
  207.8 3.5 %collective-permute-done.10 = bf16[256,256]{1,0:T(8,128)(2,1)S(1)} collective-permute-done((bf16[256,256]{1,0:T(8,128)(2,1)S(1)}, bf16[256,256]{1,0:T(8,128)(2,1)S(1)}, u32[]{:S(2)}, u32[]{:S(2)}) %collective-permute-start.10) | collective-permute-done | bytes 131104 | tf_op jit(solution)/shard_map/ppermute | solution.py:12
  212.4 5.3 %collective-permute-start.13 = (bf16[256,256]{1,0:T(8,128)(2,1)S(1)}, bf16[256,256]{1,0:T(8,128)(2,1)S(1)}, u32[]{:S(2)}, u32[]{:S(2)}) collective-permute-start(bf16[256,256]{1,0:T(8,128)(2,1)S(1)} %get-tuple-element.21), channel_id=1, source_target_pairs={{0,31},{1,0},{2,1},{3,2},{4,3},{5,4},{6,5},{7,6},{8,7},{9,8},{10,9... | collective-permute-start | bytes 393224 | tf_op jit(solution)/shard_map/ppermute | solution.py:12
  218.2 2.7 %collective-permute-done.12 = bf16[256,256]{1,0:T(8,128)(2,1)S(1)} collective-permute-done((bf16[256,256]{1,0:T(8,128)(2,1)S(1)}, bf16[256,256]{1,0:T(8,128)(2,1)S(1)}, u32[]{:S(2)}, u32[]{:S(2)}) %collective-permute-start.12) | collective-permute-done | bytes 131104 | tf_op jit(solution)/shard_map/ppermute | solution.py:12
  (128 shorter events, 33.7 us)
Async XLA Ops:
  7.2 112.9 %all-gather.3.cloned.1.call-start = ((), (), s32[]{:S(2)}) async-start(), calls=%async_computation.2 | async-start | bytes 1179648 | tf_op jit(solution)/shard_map/all_gather | solution.py:29
  31.1 20.8 %collective-permute-start = (bf16[256,256]{1,0:T(8,128)(2,1)}, bf16[256,256]{1,0:T(8,128)(2,1)S(1)}, u32[]{:S(2)}, u32[]{:S(2)}) collective-permute-start(bf16[256,256]{1,0:T(8,128)(2,1)} %get-tuple-element.34), channel_id=1, source_target_pairs={{0,1},{1,2},{2,3},{3,4},{4,5},{5,6},{6,7},{7,8},{8,9},{9,10},{10,1... | collective-permute-start | bytes 393224 | tf_op jit(solution)/shard_map/ppermute | solution.py:12
  34.1 17.8 %collective-permute-start.1 = (bf16[256,256]{1,0:T(8,128)(2,1)S(1)}, bf16[256,256]{1,0:T(8,128)(2,1)S(1)}, u32[]{:S(2)}, u32[]{:S(2)}) collective-permute-start(bf16[256,256]{1,0:T(8,128)(2,1)S(1)} %get-tuple-element.33), channel_id=1, source_target_pairs={{0,31},{1,0},{2,1},{3,2},{4,3},{5,4},{6,5},{7,6},{8,7},{9,8},{10,9... | collective-permute-start | bytes 393224 | tf_op jit(solution)/shard_map/ppermute | solution.py:12
  54.2 9.5 %copy-start.7 = (s32[1,1024,512]{1,2,0:T(8,128)S(1)}, s32[1,1024,512]{1,2,0:T(8,128)}, u32[]{:S(2)}) copy-start(s32[1,1024,512]{1,2,0:T(8,128)} %copy.72) | copy-start | bytes 6291460
  54.2 9.5 %copy-start.17 = (bf16[1,1024,512]{1,2,0:T(8,128)(2,1)S(1)}, bf16[1,1024,512]{1,2,0:T(8,128)(2,1)}, u32[]{:S(2)}) copy-start(bf16[1,1024,512]{1,2,0:T(8,128)(2,1)} %copy.73) | copy-start | bytes 3145732
  54.2 9.4 %collective-permute-start.2 = (bf16[256,256]{1,0:T(8,128)(2,1)S(1)}, bf16[256,256]{1,0:T(8,128)(2,1)S(1)}, u32[]{:S(2)}, u32[]{:S(2)}) collective-permute-start(bf16[256,256]{1,0:T(8,128)(2,1)S(1)} %get-tuple-element.32), channel_id=1, source_target_pairs={{0,1},{1,2},{2,3},{3,4},{4,5},{5,6},{6,7},{7,8},{8,9},{9,10},{10,1... | collective-permute-start | bytes 393224 | tf_op jit(solution)/shard_map/ppermute | solution.py:12
  54.3 9.3 %collective-permute-start.3 = (bf16[256,256]{1,0:T(8,128)(2,1)S(1)}, bf16[256,256]{1,0:T(8,128)(2,1)S(1)}, u32[]{:S(2)}, u32[]{:S(2)}) collective-permute-start(bf16[256,256]{1,0:T(8,128)(2,1)S(1)} %get-tuple-element.31), channel_id=1, source_target_pairs={{0,31},{1,0},{2,1},{3,2},{4,3},{5,4},{6,5},{7,6},{8,7},{9,8},{10,9... | collective-permute-start | bytes 393224 | tf_op jit(solution)/shard_map/ppermute | solution.py:12
  64.6 8.9 %copy-start.5 = (s32[1,1024,512]{1,2,0:T(8,128)S(1)}, s32[1,1024,512]{1,2,0:T(8,128)}, u32[]{:S(2)}) copy-start(s32[1,1024,512]{1,2,0:T(8,128)} %copy.74) | copy-start | bytes 6291460
  64.7 8.9 %copy-start.15 = (bf16[1,1024,512]{1,2,0:T(8,128)(2,1)S(1)}, bf16[1,1024,512]{1,2,0:T(8,128)(2,1)}, u32[]{:S(2)}) copy-start(bf16[1,1024,512]{1,2,0:T(8,128)(2,1)} %copy.75) | copy-start | bytes 3145732
  64.7 8.8 %collective-permute-start.4 = (bf16[256,256]{1,0:T(8,128)(2,1)S(1)}, bf16[256,256]{1,0:T(8,128)(2,1)S(1)}, u32[]{:S(2)}, u32[]{:S(2)}) collective-permute-start(bf16[256,256]{1,0:T(8,128)(2,1)S(1)} %get-tuple-element.30), channel_id=1, source_target_pairs={{0,1},{1,2},{2,3},{3,4},{4,5},{5,6},{6,7},{7,8},{8,9},{9,10},{10,1... | collective-permute-start | bytes 393224 | tf_op jit(solution)/shard_map/ppermute | solution.py:12
  64.7 8.7 %collective-permute-start.5 = (bf16[256,256]{1,0:T(8,128)(2,1)S(1)}, bf16[256,256]{1,0:T(8,128)(2,1)S(1)}, u32[]{:S(2)}, u32[]{:S(2)}) collective-permute-start(bf16[256,256]{1,0:T(8,128)(2,1)S(1)} %get-tuple-element.29), channel_id=1, source_target_pairs={{0,31},{1,0},{2,1},{3,2},{4,3},{5,4},{6,5},{7,6},{8,7},{9,8},{10,9... | collective-permute-start | bytes 393224 | tf_op jit(solution)/shard_map/ppermute | solution.py:12
  74.0 15.1 %copy-start.23 = (s32[2,32]{1,0:T(2,128)S(1)}, s32[2,32]{1,0:T(2,128)}, u32[]{:S(2)}) copy-start(s32[2,32]{1,0:T(2,128)} %param.11) | copy-start | bytes 772
  74.5 8.1 %collective-permute-start.6 = (bf16[256,256]{1,0:T(8,128)(2,1)S(1)}, bf16[256,256]{1,0:T(8,128)(2,1)S(1)}, u32[]{:S(2)}, u32[]{:S(2)}) collective-permute-start(bf16[256,256]{1,0:T(8,128)(2,1)S(1)} %get-tuple-element.27), channel_id=1, source_target_pairs={{0,1},{1,2},{2,3},{3,4},{4,5},{5,6},{6,7},{7,8},{8,9},{9,10},{10,1... | collective-permute-start | bytes 393224 | tf_op jit(solution)/shard_map/ppermute | solution.py:12
  83.3 78.3 %all-gather.5.cloned.1.call-start = ((), (), s32[]{:S(2)}) async-start(), calls=%async_computation.3 | async-start | bytes 1179648 | tf_op jit(solution)/shard_map/all_gather | solution.py:30
  83.4 5.0 %collective-permute-start.7 = (bf16[256,256]{1,0:T(8,128)(2,1)S(1)}, bf16[256,256]{1,0:T(8,128)(2,1)S(1)}, u32[]{:S(2)}, u32[]{:S(2)}) collective-permute-start(bf16[256,256]{1,0:T(8,128)(2,1)S(1)} %get-tuple-element.28), channel_id=1, source_target_pairs={{0,31},{1,0},{2,1},{3,2},{4,3},{5,4},{6,5},{7,6},{8,7},{9,8},{10,9... | collective-permute-start | bytes 393224 | tf_op jit(solution)/shard_map/ppermute | solution.py:12
  122.9 41.7 %all-to-all-start = ((bf16[4,256,256]{2,1,0:T(8,128)(2,1)}), bf16[4,256,256]{2,1,0:T(8,128)(2,1)S(1)}, u32[]{:S(2)}, u32[]{:S(2)}) async-start(bf16[4,256,256]{2,1,0:T(8,128)(2,1)} %copy.47), calls=%async_computation | async-start | bytes 1048576 | tf_op jit(solution)/shard_map/all_to_all | solution.py:45
  164.5 4.3 %copy-start.18 = (bf16[4,256,256]{2,1,0:T(8,128)(2,1)}, bf16[4,256,256]{2,1,0:T(8,128)(2,1)S(1)}, u32[]{:S(2)}) copy-start(bf16[4,256,256]{2,1,0:T(8,128)(2,1)S(1)} %all-to-all-done) | copy-start | bytes 1572868
  164.6 23.3 %all-to-all-start.1 = ((bf16[4,256,256]{2,1,0:T(8,128)(2,1)}), bf16[4,256,256]{2,1,0:T(8,128)(2,1)}, u32[]{:S(2)}, u32[]{:S(2)}) async-start(bf16[4,256,256]{2,1,0:T(8,128)(2,1)} %copy.49), calls=%async_computation.1 | async-start | bytes 1048576 | tf_op jit(solution)/shard_map/all_to_all | solution.py:46
  173.2 3.0 %copy-start.11 = (bf16[1,1024,512]{2,1,0:T(8,128)(2,1)S(1)}, bf16[1,1024,512]{2,1,0:T(8,128)(2,1)}, u32[]{:S(2)}) copy-start(bf16[1,1024,512]{2,1,0:T(8,128)(2,1)} %get-tuple-element.13) | copy-start | bytes 3145732
  177.6 3.0 %copy-start.10 = (bf16[1,1024,512]{2,1,0:T(8,128)(2,1)S(1)}, bf16[1,1024,512]{2,1,0:T(8,128)(2,1)}, u32[]{:S(2)}) copy-start(bf16[1,1024,512]{2,1,0:T(8,128)(2,1)} %get-tuple-element.12) | copy-start | bytes 3145732
  191.8 9.0 %copy-start.6 = (s32[1,1024,512]{1,2,0:T(8,128)S(1)}, s32[1,1024,512]{1,2,0:T(8,128)}, u32[]{:S(2)}) copy-start(s32[1,1024,512]{1,2,0:T(8,128)} %copy.78) | copy-start | bytes 6291460
  191.8 9.0 %copy-start.16 = (bf16[1,1024,512]{1,2,0:T(8,128)(2,1)S(1)}, bf16[1,1024,512]{1,2,0:T(8,128)(2,1)}, u32[]{:S(2)}) copy-start(bf16[1,1024,512]{1,2,0:T(8,128)(2,1)} %copy.79) | copy-start | bytes 3145732
  191.9 9.0 %collective-permute-start.8 = (bf16[256,256]{1,0:T(8,128)(2,1)S(1)}, bf16[256,256]{1,0:T(8,128)(2,1)S(1)}, u32[]{:S(2)}, u32[]{:S(2)}) collective-permute-start(bf16[256,256]{1,0:T(8,128)(2,1)S(1)} %get-tuple-element.26), channel_id=1, source_target_pairs={{0,1},{1,2},{2,3},{3,4},{4,5},{5,6},{6,7},{7,8},{8,9},{9,10},{10,1... | collective-permute-start | bytes 393224 | tf_op jit(solution)/shard_map/ppermute | solution.py:12
  192.5 8.4 %collective-permute-start.9 = (bf16[256,256]{1,0:T(8,128)(2,1)S(1)}, bf16[256,256]{1,0:T(8,128)(2,1)S(1)}, u32[]{:S(2)}, u32[]{:S(2)}) collective-permute-start(bf16[256,256]{1,0:T(8,128)(2,1)S(1)} %get-tuple-element.25), channel_id=1, source_target_pairs={{0,31},{1,0},{2,1},{3,2},{4,3},{5,4},{6,5},{7,6},{8,7},{9,8},{10,9... | collective-permute-start | bytes 393224 | tf_op jit(solution)/shard_map/ppermute | solution.py:12
  201.9 9.4 %copy-start.4 = (s32[1,1024,512]{1,2,0:T(8,128)S(1)}, s32[1,1024,512]{1,2,0:T(8,128)}, u32[]{:S(2)}) copy-start(s32[1,1024,512]{1,2,0:T(8,128)} %copy.80) | copy-start | bytes 6291460
  201.9 9.4 %copy-start.14 = (bf16[1,1024,512]{1,2,0:T(8,128)(2,1)S(1)}, bf16[1,1024,512]{1,2,0:T(8,128)(2,1)}, u32[]{:S(2)}) copy-start(bf16[1,1024,512]{1,2,0:T(8,128)(2,1)} %copy.81) | copy-start | bytes 3145732
  201.9 9.3 %collective-permute-start.10 = (bf16[256,256]{1,0:T(8,128)(2,1)S(1)}, bf16[256,256]{1,0:T(8,128)(2,1)S(1)}, u32[]{:S(2)}, u32[]{:S(2)}) collective-permute-start(bf16[256,256]{1,0:T(8,128)(2,1)S(1)} %get-tuple-element.24), channel_id=1, source_target_pairs={{0,1},{1,2},{2,3},{3,4},{4,5},{5,6},{6,7},{7,8},{8,9},{9,10},{10,1... | collective-permute-start | bytes 393224 | tf_op jit(solution)/shard_map/ppermute | solution.py:12
  202.1 9.2 %collective-permute-start.11 = (bf16[256,256]{1,0:T(8,128)(2,1)S(1)}, bf16[256,256]{1,0:T(8,128)(2,1)S(1)}, u32[]{:S(2)}, u32[]{:S(2)}) collective-permute-start(bf16[256,256]{1,0:T(8,128)(2,1)S(1)} %get-tuple-element.23), channel_id=1, source_target_pairs={{0,31},{1,0},{2,1},{3,2},{4,3},{5,4},{6,5},{7,6},{8,7},{9,8},{10,9... | collective-permute-start | bytes 393224 | tf_op jit(solution)/shard_map/ppermute | solution.py:12
  212.3 8.6 %copy-start.3 = (s32[1,1024,512]{1,2,0:T(8,128)S(1)}, s32[1,1024,512]{1,2,0:T(8,128)}, u32[]{:S(2)}) copy-start(s32[1,1024,512]{1,2,0:T(8,128)} %copy.82) | copy-start | bytes 6291460
  212.3 8.6 %copy-start.13 = (bf16[1,1024,512]{1,2,0:T(8,128)(2,1)S(1)}, bf16[1,1024,512]{1,2,0:T(8,128)(2,1)}, u32[]{:S(2)}) copy-start(bf16[1,1024,512]{1,2,0:T(8,128)(2,1)} %copy.83) | copy-start | bytes 3145732
  212.3 8.5 %collective-permute-start.12 = (bf16[256,256]{1,0:T(8,128)(2,1)S(1)}, bf16[256,256]{1,0:T(8,128)(2,1)S(1)}, u32[]{:S(2)}, u32[]{:S(2)}) collective-permute-start(bf16[256,256]{1,0:T(8,128)(2,1)S(1)} %get-tuple-element.22), channel_id=1, source_target_pairs={{0,1},{1,2},{2,3},{3,4},{4,5},{5,6},{6,7},{7,8},{8,9},{9,10},{10,1... | collective-permute-start | bytes 393224 | tf_op jit(solution)/shard_map/ppermute | solution.py:12
  212.4 8.5 %collective-permute-start.13 = (bf16[256,256]{1,0:T(8,128)(2,1)S(1)}, bf16[256,256]{1,0:T(8,128)(2,1)S(1)}, u32[]{:S(2)}, u32[]{:S(2)}) collective-permute-start(bf16[256,256]{1,0:T(8,128)(2,1)S(1)} %get-tuple-element.21), channel_id=1, source_target_pairs={{0,31},{1,0},{2,1},{3,2},{4,3},{5,4},{6,5},{7,6},{8,7},{9,8},{10,9... | collective-permute-start | bytes 393224 | tf_op jit(solution)/shard_map/ppermute | solution.py:12
  (10 other events, 17.9 us)
Sparse Core Ops, SparseCore 0:
  83.4 36.5 all-gather.2
  122.7 38.8 all-gather.4
where the time goes:
time: 231 us
  waiting for transfers between devices  94.3 us (41%)
  local copies, waits for them, and re-layouts  56.7 us (25%)
  starting transfers between devices  41.8 us (18%)
  matrix products  21.1 us (9%)
  between operations  14.7 us (6%)
    unnamed x71, local copies, waits for them, and re-layouts  35.8 us
    all_gather x1, waiting for transfers between devices, body(): lax.all_gather(behind, 'blk', axis=0, tiled=True)  35.2 us
    ppermute x14, starting transfers between devices, from_behind(): lax.ppermute(array, axis, [(i, (i + by) % count) for i in range(count)])  33.9 us
    all_gather x1, waiting for transfers between devices, body(): lax.all_gather(ahead, 'blk', axis=0, tiled=True)  30.8 us
    ppermute x14, waiting for transfers between devices, from_behind(): lax.ppermute(array, axis, [(i, (i + by) % count) for i in range(count)])  28.2 us
    slice x1, local copies, waits for them, and re-layouts, body(): rated[stratum] == 1  11.5 us
    dot_general x8, matrix products, body(): lax.dot_general(user_b, block, (((1,), (1,)), ((), ())), preferred_elemen...  8.73 us
    slice x1, local copies, waits for them, and re-layouts, body(): ratings[stratum].astype(jnp.float32)  5.94 us
  transfers between devices with their start and end apart: 18, of which 9 were waited for; matrix products, arithmetic and copies ran while one was open for 18% of the time, Pallas kernels for 0%

commit v1 on v0

v1 whole, which is shorter than its diff:
```python
import functools

import jax
import jax.numpy as jnp
from jax import lax
from jax.experimental import pallas as pl
from jax.experimental.pallas import tpu as pltpu
from jax.sharding import PartitionSpec as P

RATE = 0.005
DECAY = 0.05
TABLES = 2
PARTS = 4
MESH = pl.DeviceIdType.MESH


def line_split(columns):
    inner = 1
    while columns % (inner * inner * 4) == 0 or (columns % (inner * 2) == 0 and inner * inner * 4 <= columns):
        inner *= 2
    return columns // inner, inner


def kernel(
    groups, columns, strata,
    ratings, rated, users_in, ahead_in, behind_in, owners,
    users, ahead_out, behind_out,
    rate_buf, mask_buf, q_in, q_out, user_b, err,
    *rest,
):
    gath = rest[:PARTS]
    outb = rest[PARTS:2 * PARTS]
    fin = rest[2 * PARTS:3 * PARTS]
    (rate_sem, mask_sem, ring_send, ring_recv, core_send, core_recv,
     line_send, line_recv, all_send, all_recv) = rest[3 * PARTS:]

    count = groups * columns
    line, inner = line_split(columns)
    pairs = groups // TABLES
    mid = strata // 2
    half = ahead_in.shape[0]
    rows = half // PARTS

    g = lax.axis_index("grp")
    b = lax.axis_index("blk")
    me = g * columns + b
    c = lax.rem(g, TABLES)
    y = lax.div(g, TABLES)
    z = lax.div(b, inner)
    x = lax.rem(b, inner)

    def load_rate(s):
        return pltpu.make_async_copy(ratings.at[s], rate_buf.at[s], rate_sem.at[s])

    def load_mask(s):
        return pltpu.make_async_copy(rated.at[s], mask_buf.at[s], mask_sem.at[s])

    def at(d):
        return (lax.div(d, columns), lax.rem(d, columns))

    after = at(lax.rem(me + 1, count))
    before = at(lax.rem(me + count - 1, count))
    mate = (y * TABLES + (TABLES - 1 - c), b)
    up = (g, jnp.minimum(z + 1, line - 1) * inner + x)
    down = (g, jnp.maximum(z - 1, 0) * inner + x)
    offsets = [
        (dy, dx, dc)
        for dy in range(pairs) for dx in range(inner) for dc in range(TABLES)
        if (dy, dx, dc) != (0, 0, 0)
    ]

    def peer(dy, dx, dc):
        return (
            lax.rem(y + dy, pairs) * TABLES + lax.rem(c + dc, TABLES),
            z * inner + lax.rem(x + dx, inner),
        )

    barrier = pltpu.get_barrier_semaphore()

    def greet(device):
        pl.semaphore_signal(barrier, inc=1, device_id=device, device_id_type=MESH)

    greet(after)
    greet(before)
    for o in offsets:
        greet(peer(*o))

    @pl.when(z + 1 < line)
    def _():
        greet(up)

    @pl.when(z > 0)
    def _():
        greet(down)

    def issue(s, carry):
        load_rate(s).start()
        load_mask(s).start()
        return carry

    lax.fori_loop(0, strata, issue, 0)

    q_in[0, 0] = ahead_in[...]
    q_in[0, 1] = behind_in[...]
    users[...] = users_in[...]
    user_b[...] = users_in[...].astype(jnp.bfloat16)

    greeted = 2 + len(offsets)
    greeted = greeted + jnp.where(z + 1 < line, 1, 0) + jnp.where(z > 0, 1, 0)
    pl.semaphore_wait(barrier, greeted)

    def ring(s, t):
        return pltpu.make_async_remote_copy(
            src_ref=q_out.at[s, t], dst_ref=q_in.at[s + 1, t],
            send_sem=ring_send.at[s, t], recv_sem=ring_recv.at[s + 1, t],
            device_id=after if t == 0 else before, device_id_type=MESH,
        )

    def ring_arrival(s, t):
        return pltpu.make_async_remote_copy(
            src_ref=q_out.at[s, t], dst_ref=q_in.at[s, t],
            send_sem=ring_send.at[s, t], recv_sem=ring_recv.at[s, t],
            device_id=after if t == 0 else before, device_id_type=MESH,
        )

    own = z * TABLES + c

    def mate_copy(p):
        return pltpu.make_async_remote_copy(
            src_ref=q_out.at[mid - 1, TABLES - 1 - c, pl.ds(p * rows, rows)],
            dst_ref=gath[p].at[own],
            send_sem=core_send.at[p], recv_sem=core_recv.at[p],
            device_id=mate, device_id_type=MESH,
        )

    def line_copy(p, k, way):
        src = z - k if way == 0 else z + k
        slot = gath[p].at[pl.ds(src * TABLES, TABLES)]
        return pltpu.make_async_remote_copy(
            src_ref=slot, dst_ref=slot,
            send_sem=line_send.at[p, k, way], recv_sem=line_recv.at[p, k, way],
            device_id=up if way == 0 else down, device_id_type=MESH,
        )

    def line_sends(k, way):
        if way == 0:
            return jnp.logical_and(z - k >= 0, z + 1 < line)
        return jnp.logical_and(z + k < line, z > 0)

    def line_arrival(p, k, way):
        src = z - k - 1 if way == 0 else z + k + 1
        slot = gath[p].at[pl.ds(src * TABLES, TABLES)]
        return pltpu.make_async_remote_copy(
            src_ref=slot, dst_ref=slot,
            send_sem=line_send.at[p, k, way], recv_sem=line_recv.at[p, k, way],
            device_id=up if way == 0 else down, device_id_type=MESH,
        )

    def line_gets(k, way):
        return z - k - 1 >= 0 if way == 0 else z + k + 1 < line

    chips = pairs * inner
    chip = y * inner + x

    def all_copy(p, i):
        return pltpu.make_async_remote_copy(
            src_ref=outb[p].at[i], dst_ref=fin[p].at[c * chips + chip],
            send_sem=all_send.at[p, i], recv_sem=all_recv.at[p, i],
            device_id=peer(*offsets[i]), device_id_type=MESH,
        )

    def all_arrival(p, i):
        dy, dx, dc = offsets[i]
        source = lax.rem(y + pairs - dy, pairs) * inner + lax.rem(x + inner - dx, inner)
        return pltpu.make_async_remote_copy(
            src_ref=outb[p].at[i],
            dst_ref=fin[p].at[lax.rem(c + TABLES - dc, TABLES) * chips + source],
            send_sem=all_send.at[p, i], recv_sem=all_recv.at[p, i],
            device_id=peer(*offsets[i]), device_id_type=MESH,
        )

    def exchange():
        for p in range(PARTS):
            mate_copy(p).start()
            gath[p][own] = q_out[mid - 1, c, pl.ds(p * rows, rows)]
        step = jnp.where(c == 0, 1, count - 1)
        holders = []
        for zs in range(line):
            for cs in range(TABLES):
                src = (y * TABLES + cs) * columns + zs * inner + x
                holders.append(owners[c, lax.rem(src + step, count)])

        def pick(device):
            target = device[0] * columns + device[1]
            j = jnp.int32(0)
            for k, holder in enumerate(holders):
                j = jnp.where(holder == target, k, j)
            return j

        picks = [pick(peer(*o)) for o in offsets]
        self_pick = pick((g, b))
        origin = []
        for t in range(TABLES):
            found = jnp.int32(0)
            for src in range(count):
                sg, sb = divmod(src, columns)
                shifted = (src + (1 if t == 0 else count - 1)) % count
                found = jnp.where(
                    owners[t, shifted] == me, (sg // TABLES) * inner + sb % inner, found
                )
            origin.append(t * chips + found)

        def advance(p, k):
            if k == 0:
                arrived = pltpu.make_async_remote_copy(
                    src_ref=q_out.at[mid - 1, TABLES - 1 - c, pl.ds(p * rows, rows)],
                    dst_ref=gath[p].at[z * TABLES + (TABLES - 1 - c)],
                    send_sem=core_send.at[p], recv_sem=core_recv.at[p],
                    device_id=mate, device_id_type=MESH,
                )
                arrived.wait_recv()
            else:
                for way in range(2):
                    @pl.when(line_gets(k - 1, way))
                    def _():
                        line_arrival(p, k - 1, way).wait_recv()
            if k < line - 1:
                for way in range(2):
                    @pl.when(line_sends(k, way))
                    def _():
                        line_copy(p, k, way).start()
            else:
                for i in range(len(offsets)):
                    outb[p][i] = gath[p][picks[i]]
                    all_copy(p, i).start()
                fin[p][c * chips + chip] = gath[p][self_pick]

        for wave in range(PARTS + line - 1):
            for p in range(PARTS):
                if 0 <= wave - p < line:
                    advance(p, wave - p)
        for p in range(PARTS):
            for i in range(len(offsets)):
                all_arrival(p, i).wait_recv()
            for t in range(TABLES):
                q_in[mid, t, pl.ds(p * rows, rows)] = fin[p][origin[t]]
        for p in range(PARTS):
            mate_copy(p).wait_send()
            for k in range(line - 1):
                for way in range(2):
                    @pl.when(line_sends(k, way))
                    def _():
                        line_copy(p, k, way).wait_send()
            for i in range(len(offsets)):
                all_copy(p, i).wait_send()

    def stratum(s, carry):
        @pl.when(s == mid)
        def _():
            exchange()

        load_rate(s).wait()
        load_mask(s).wait()
        for t in range(TABLES):
            @pl.when(jnp.logical_and(s > 0, s != mid))
            def _():
                ring_arrival(s, t).wait_recv()

            block = q_in[s, t]
            part = slice(t * half, (t + 1) * half)
            pred = lax.dot_general(
                user_b[...], block, (((1,), (1,)), ((), ())),
                preferred_element_type=jnp.float32,
            )
            err[:, part] = jnp.where(
                mask_buf[s, :, part] == 1,
                pred - rate_buf[s, :, part].astype(jnp.float32), 0.0,
            ).astype(jnp.bfloat16)
            grad_item = lax.dot_general(
                err[:, part], user_b[...], (((0,), (0,)), ((), ())),
                preferred_element_type=jnp.float32,
            )
            block_f = block.astype(jnp.float32)
            q_out[s, t] = (
                block_f - RATE * (grad_item + DECAY * block_f)
            ).astype(jnp.bfloat16)

            @pl.when(jnp.logical_and(s < strata - 1, s != mid - 1))
            def _():
                ring(s, t).start()

        grad_user = jnp.dot(
            err[...], q_in[s].reshape(TABLES * half, -1), preferred_element_type=jnp.float32
        )
        old = users[...]
        new = old - RATE * (grad_user + DECAY * old)
        users[...] = new
        user_b[...] = new.astype(jnp.bfloat16)
        return carry

    lax.fori_loop(0, strata, stratum, 0)
    ahead_out[...] = q_out[strata - 1, 0]
    behind_out[...] = q_out[strata - 1, 1]

    def drain(s, carry):
        @pl.when(s != mid - 1)
        def _():
            for t in range(TABLES):
                ring(s, t).wait_send()
        return carry

    lax.fori_loop(0, strata - 1, drain, 0)


def body(ratings, rated, user_factors, item_ahead, item_behind, owners):
    groups = lax.axis_size("grp")
    columns = lax.axis_size("blk")
    strata, own_users, items = ratings.shape
    half, rank = item_ahead.shape
    rows = half // PARTS
    line, inner = line_split(columns)
    chips = (groups // TABLES) * inner
    peers = chips * TABLES - 1
    vmem = pl.BlockSpec(memory_space=pltpu.VMEM)
    anywhere = pl.BlockSpec(memory_space=pl.ANY)
    bf16 = jnp.bfloat16
    dma = pltpu.SemaphoreType.DMA
    scratch = (
        [
            pltpu.VMEM((strata, own_users, items), ratings.dtype),
            pltpu.VMEM((strata, own_users, items), rated.dtype),
            pltpu.VMEM((strata, TABLES, half, rank), bf16),
            pltpu.VMEM((strata, TABLES, half, rank), bf16),
            pltpu.VMEM((own_users, rank), bf16),
            pltpu.VMEM((own_users, items), bf16),
        ]
        + [pltpu.VMEM((line * TABLES, rows, rank), bf16)] * PARTS
        + [pltpu.VMEM((peers, rows, rank), bf16)] * PARTS
        + [pltpu.VMEM((TABLES * chips, rows, rank), bf16)] * PARTS
        + [
            dma((strata,)), dma((strata,)),
            dma((strata, TABLES)), dma((strata, TABLES)),
            dma((PARTS,)), dma((PARTS,)),
            dma((PARTS, line - 1, 2)), dma((PARTS, line - 1, 2)),
            dma((PARTS, peers)), dma((PARTS, peers)),
        ]
    )
    return pl.pallas_call(
        functools.partial(kernel, groups, columns, strata),
        out_shape=(
            jax.ShapeDtypeStruct(user_factors.shape, jnp.float32),
            jax.ShapeDtypeStruct(item_ahead.shape, bf16),
            jax.ShapeDtypeStruct(item_behind.shape, bf16),
        ),
        in_specs=[anywhere, anywhere, vmem, vmem, vmem,
                  pl.BlockSpec(memory_space=pltpu.SMEM)],
        out_specs=(vmem, vmem, vmem),
        scratch_shapes=scratch,
        compiler_params=pltpu.CompilerParams(
            collective_id=0, has_side_effects=True, vmem_limit_bytes=56 * 1024 * 1024
        ),
        cost_estimate=pl.CostEstimate(
            flops=6 * strata * own_users * items * rank,
            bytes_accessed=6 * strata * own_users * items, transcendentals=0,
        ),
    )(ratings, rated, user_factors, item_ahead, item_behind, owners)


def solution(mesh):
    shard = P(("grp", "blk"), None)
    strata = P(None, ("grp", "blk"), None)
    return jax.shard_map(
        body, mesh=mesh,
        in_specs=(strata, strata, shard, shard, shard, P()),
        out_specs=(shard, shard, shard), check_vma=False,
    )
```

time: 231 us -> 93.3 us (0.40)
  waiting for transfers between devices: 94.3 us -> 0 us
  Pallas kernels: 0 us -> 87 us
  local copies, waits for them, and re-layouts: 56.7 us -> 5.4 us
  starting transfers between devices: 41.8 us -> 0 us
  matrix products: 21.1 us -> 0 us
  between operations: 14.7 us -> 0.64 us
    pallas_call x0 -> x1, Pallas kernels: none -> 87 us  [body(): pl.pallas_call(functools.partial(kernel, groups, columns, strata), out_sh...]
    all_gather x2 -> x0, waiting for transfers between devices: 66 us -> none  [the longest x1 35.2 us: body(): lax.all_gather(behind, 'blk', axis=0, tiled=True)]
    ppermute x14 -> x0, starting transfers between devices: 33.9 us -> none  [from_behind(): lax.ppermute(array, axis, [(i, (i + by) % count) for i in range(count)])]
    unnamed x71 -> x3, local copies, waits for them, and re-layouts: 35.8 us -> 5.4 us
    ppermute x14 -> x0, waiting for transfers between devices: 28.2 us -> none  [from_behind(): lax.ppermute(array, axis, [(i, (i + by) % count) for i in range(count)])]
    dot_general x26 -> x0, matrix products: 21.1 us -> none  [the longest x8 8.73 us: body(): lax.dot_general(user_b, block, (((1,), (1,)), ((), ())), preferred_elemen...]
    slice x11 -> x0, local copies, waits for them, and re-layouts: 18.9 us -> none  [the longest x1 11.5 us: body(): rated[stratum] == 1]
    all_to_all x2 -> x0, starting transfers between devices: 7.79 us -> none  [the longest x1 4.32 us: body(): lax.all_to_all(send_b, 'grp', split_axis=0, concat_axis=0, tiled=True)]
  transfers between devices with their start and end apart: 18 -> 0, of which waited for: 9 -> 0; matrix products, arithmetic and copies ran while one was open for 18% -> 0% of each run, Pallas kernels for 0% -> 0%
where the time goes in v1:
time: 93.3 us; the launch traced here: 93 us
  Pallas kernels  87 us (93%)
  local copies, waits for them, and re-layouts  5.4 us (6%)
    pallas_call x1, Pallas kernels, body(): pl.pallas_call(functools.partial(kernel, groups, columns, strata), out_sh...  87 us
    unnamed x3, local copies, waits for them, and re-layouts  5.4 us

profile of v1, /device:TPU:0, one launch (start us, length us, event | category | flops | bytes accessed | tf_op | source)
XLA Modules:
  0.0 93.0 jit_solution(3284304581627455932)
XLA Ops:
  0.6 87.0 %shard_map.85 = (f32[1024,256]{1,0:T(8,128)}, bf16[256,256]{1,0:T(8,128)(2,1)}, bf16[256,256]{1,0:T(8,128)(2,1)}) custom-call(bf16[8,1024,512]{2,1,0:T(8,128)(2,1)} %ratings.1, s32[8,1024,512]{2,1,0:T(8,128)} %rated.1, f32[1024,256]{1,0:T(8,128)} %users_in.1, bf16[256,256]{1,0:T(8,128)(2,1)} %ahead_in.1, bf16[256,256]{1,0:T(8,128)(2,1)} %behind_in.1, ...), custom_call_target="tpu_custom_call" | custom-call | flops 6442450944 | bytes 25165824 | tf_op jit(solution)/shard_map/pallas_call | solution.py:348
  87.6 2.3 %copy.12 = f32[1024,256]{1,0:T(8,128)} copy(f32[1024,256]{1,0:T(8,128)} %get-tuple-element.6) | data formatting | bytes 2097152
  89.9 1.6 %copy.13 = bf16[256,256]{1,0:T(8,128)(2,1)} copy(bf16[256,256]{1,0:T(8,128)(2,1)} %get-tuple-element.7) | data formatting | bytes 262144
  91.4 1.6 %copy.14 = bf16[256,256]{1,0:T(8,128)(2,1)} copy(bf16[256,256]{1,0:T(8,128)(2,1)} %get-tuple-element.8) | data formatting | bytes 262144

commit v2 on v1

--- a/solution.py
+++ b/solution.py
@@ -10,7 +10,9 @@
 RATE = 0.005
 DECAY = 0.05
 TABLES = 2
-PARTS = 4
+AHEAD = 2
+SPLIT = 2
+PARTS = 2
 MESH = pl.DeviceIdType.MESH
 
 
@@ -25,7 +27,7 @@
     groups, columns, strata,
     ratings, rated, users_in, ahead_in, behind_in, owners,
     users, ahead_out, behind_out,
-    rate_buf, mask_buf, q_in, q_out, user_b, err,
+    rate_buf, mask_buf, q_in, q_out, user_b, err, total,
     *rest,
 ):
     gath = rest[:PARTS]
@@ -93,12 +95,13 @@
     def _():
         greet(down)
 
-    def issue(s, carry):
+    def issue(s):
         load_rate(s).start()
         load_mask(s).start()
-        return carry
-
-    lax.fori_loop(0, strata, issue, 0)
+
+    early = min(AHEAD, strata)
+    for s in range(early):
+        issue(s)
 
     q_in[0, 0] = ahead_in[...]
     q_in[0, 1] = behind_in[...]
@@ -107,19 +110,22 @@
 
     greeted = 2 + len(offsets)
     greeted = greeted + jnp.where(z + 1 < line, 1, 0) + jnp.where(z > 0, 1, 0)
-    pl.semaphore_wait(barrier, greeted)
-
-    def ring(s, t):
-        return pltpu.make_async_remote_copy(
-            src_ref=q_out.at[s, t], dst_ref=q_in.at[s + 1, t],
-            send_sem=ring_send.at[s, t], recv_sem=ring_recv.at[s + 1, t],
+
+    piece = half // SPLIT
+
+    def ring(s, t, i):
+        span = pl.ds(i * piece, piece)
+        return pltpu.make_async_remote_copy(
+            src_ref=q_out.at[s, t, span], dst_ref=q_in.at[s + 1, t, span],
+            send_sem=ring_send.at[s, t, i], recv_sem=ring_recv.at[s + 1, t, i],
             device_id=after if t == 0 else before, device_id_type=MESH,
         )
 
-    def ring_arrival(s, t):
-        return pltpu.make_async_remote_copy(
-            src_ref=q_out.at[s, t], dst_ref=q_in.at[s, t],
-            send_sem=ring_send.at[s, t], recv_sem=ring_recv.at[s, t],
+    def ring_arrival(s, t, i):
+        span = pl.ds(i * piece, piece)
+        return pltpu.make_async_remote_copy(
+            src_ref=q_out.at[s, t, span], dst_ref=q_in.at[s, t, span],
+            send_sem=ring_send.at[s, t, i], recv_sem=ring_recv.at[s, t, i],
             device_id=after if t == 0 else before, device_id_type=MESH,
         )
 
@@ -179,10 +185,12 @@
             device_id=peer(*offsets[i]), device_id_type=MESH,
         )
 
-    def exchange():
+    def exchange_start():
         for p in range(PARTS):
             mate_copy(p).start()
             gath[p][own] = q_out[mid - 1, c, pl.ds(p * rows, rows)]
+
+    def exchange():
         step = jnp.where(c == 0, 1, count - 1)
         holders = []
         for zs in range(line):
@@ -254,20 +262,24 @@
             for i in range(len(offsets)):
                 all_copy(p, i).wait_send()
 
+    pieces = [(i, t) for i in range(SPLIT) for t in range(TABLES)]
+
     def stratum(s, carry):
-        @pl.when(s == mid)
-        def _():
-            exchange()
-
         load_rate(s).wait()
         load_mask(s).wait()
-        for t in range(TABLES):
+
+        @pl.when(s + early < strata)
+        def _():
+            issue(s + early)
+
+        for k, (i, t) in enumerate(pieces):
             @pl.when(jnp.logical_and(s > 0, s != mid))
             def _():
-                ring_arrival(s, t).wait_recv()
-
-            block = q_in[s, t]
-            part = slice(t * half, (t + 1) * half)
+                ring_arrival(s, t, i).wait_recv()
+
+            span = slice(i * piece, (i + 1) * piece)
+            part = slice(t * half + i * piece, t * half + (i + 1) * piece)
+            block = q_in[s, t, span]
             pred = lax.dot_general(
                 user_b[...], block, (((1,), (1,)), ((), ())),
                 preferred_element_type=jnp.float32,
@@ -281,21 +293,39 @@
                 preferred_element_type=jnp.float32,
             )
             block_f = block.astype(jnp.float32)
-            q_out[s, t] = (
+            q_out[s, t, span] = (
                 block_f - RATE * (grad_item + DECAY * block_f)
             ).astype(jnp.bfloat16)
 
+            if k == 0:
+                @pl.when(s == 0)
+                def _():
+                    pl.semaphore_wait(barrier, greeted)
+
             @pl.when(jnp.logical_and(s < strata - 1, s != mid - 1))
             def _():
-                ring(s, t).start()
-
-        grad_user = jnp.dot(
-            err[...], q_in[s].reshape(TABLES * half, -1), preferred_element_type=jnp.float32
-        )
-        old = users[...]
-        new = old - RATE * (grad_user + DECAY * old)
-        users[...] = new
-        user_b[...] = new.astype(jnp.bfloat16)
+                ring(s, t, i).start()
+
+            if k == len(pieces) - 1:
+                @pl.when(s == mid - 1)
+                def _():
+                    exchange_start()
+
+            grad_user = jnp.dot(err[:, part], block, preferred_element_type=jnp.float32)
+            if k == 0:
+                total[...] = grad_user
+            elif k < len(pieces) - 1:
+                total[...] += grad_user
+            else:
+                old = users[...]
+                new = old - RATE * (total[...] + grad_user + DECAY * old)
+                users[...] = new
+                user_b[...] = new.astype(jnp.bfloat16)
+
+        @pl.when(s == mid - 1)
+        def _():
+            exchange()
+
         return carry
 
     lax.fori_loop(0, strata, stratum, 0)
@@ -305,11 +335,25 @@
     def drain(s, carry):
         @pl.when(s != mid - 1)
         def _():
-            for t in range(TABLES):
-                ring(s, t).wait_send()
+            for i, t in pieces:
+                ring(s, t, i).wait_send()
         return carry
 
     lax.fori_loop(0, strata - 1, drain, 0)
+
+
+def settle(arrays):
+    shapes = tuple(jax.ShapeDtypeStruct(a.shape, a.dtype) for a in arrays)
+    n = len(arrays)
+    where = pl.BlockSpec(memory_space=pltpu.VMEM)
+
+    def copies(*refs):
+        for i in range(n):
+            refs[n + i][...] = refs[i][...]
+
+    return pl.pallas_call(
+        copies, out_shape=shapes, in_specs=[where] * n, out_specs=(where,) * n,
+    )(*arrays)
 
 
 def body(ratings, rated, user_factors, item_ahead, item_behind, owners):
@@ -333,19 +377,20 @@
             pltpu.VMEM((strata, TABLES, half, rank), bf16),
             pltpu.VMEM((own_users, rank), bf16),
             pltpu.VMEM((own_users, items), bf16),
+            pltpu.VMEM((own_users, rank), jnp.float32),
         ]
         + [pltpu.VMEM((line * TABLES, rows, rank), bf16)] * PARTS
         + [pltpu.VMEM((peers, rows, rank), bf16)] * PARTS
         + [pltpu.VMEM((TABLES * chips, rows, rank), bf16)] * PARTS
         + [
             dma((strata,)), dma((strata,)),
-            dma((strata, TABLES)), dma((strata, TABLES)),
+            dma((strata, TABLES, SPLIT)), dma((strata, TABLES, SPLIT)),
             dma((PARTS,)), dma((PARTS,)),
             dma((PARTS, line - 1, 2)), dma((PARTS, line - 1, 2)),
             dma((PARTS, peers)), dma((PARTS, peers)),
         ]
     )
-    return pl.pallas_call(
+    moved = pl.pallas_call(
         functools.partial(kernel, groups, columns, strata),
         out_shape=(
             jax.ShapeDtypeStruct(user_factors.shape, jnp.float32),
@@ -364,6 +409,7 @@
             bytes_accessed=6 * strata * own_users * items, transcendentals=0,
         ),
     )(ratings, rated, user_factors, item_ahead, item_behind, owners)
+    return settle(moved)
 
 
 def solution(mesh):

time: 93.3 us -> 86.3 us (0.925)
  local copies, waits for them, and re-layouts: 5.4 us -> 0 us
  Pallas kernels: 87 us -> 85.4 us
    unnamed x3 -> x0, local copies, waits for them, and re-layouts: 5.4 us -> none
    pallas_call x1, Pallas kernels: 87 us -> 83.1 us  [body(): pl.pallas_call(functools.partial(kernel, groups, columns, strata), out_sh...]
    pallas_call x0 -> x1, Pallas kernels: none -> 2.38 us  [settle(): pl.pallas_call(copies, out_shape=shapes, in_specs=[where] * n, out_specs=...]
where the time goes in v2:
time: 86.3 us; the launch traced here: 86.1 us
  Pallas kernels  85.4 us (99%)
    pallas_call x1, Pallas kernels, body(): pl.pallas_call(functools.partial(kernel, groups, columns, strata), out_sh...  83.1 us
    pallas_call x1, Pallas kernels, settle(): pl.pallas_call(copies, out_shape=shapes, in_specs=[where] * n, out_specs=...  2.38 us

profile of v2, /device:TPU:0, one launch (start us, length us, event | category | flops | bytes accessed | tf_op | source)
XLA Modules:
  0.0 86.1 jit_solution(11116017751273176553)
XLA Ops:
  0.6 83.1 %shard_map.85 = (f32[1024,256]{1,0:T(8,128)}, bf16[256,256]{1,0:T(8,128)(2,1)}, bf16[256,256]{1,0:T(8,128)(2,1)}) custom-call(bf16[8,1024,512]{2,1,0:T(8,128)(2,1)} %ratings.1, s32[8,1024,512]{2,1,0:T(8,128)} %rated.1, f32[1024,256]{1,0:T(8,128)} %users_in.1, bf16[256,256]{1,0:T(8,128)(2,1)} %ahead_in.1, bf16[256,256]{1,0:T(8,128)(2,1)} %behind_in.1, ...), custom_call_target="tpu_custom_call" | custom-call | flops 6442450944 | bytes 25165824 | tf_op jit(solution)/shard_map/pallas_call | solution.py:393
  83.7 2.4 %shard_map.86 = (f32[1024,256]{1,0:T(8,128)}, bf16[256,256]{1,0:T(8,128)(2,1)}, bf16[256,256]{1,0:T(8,128)(2,1)}) custom-call(f32[1024,256]{1,0:T(8,128)} %get-tuple-element.6.refs_0_, bf16[256,256]{1,0:T(8,128)(2,1)} %get-tuple-element.7.refs_1_, bf16[256,256]{1,0:T(8,128)(2,1)} %get-tuple-element.8.refs_2_), custom_call_target="tpu_custom_call" | custom-call | tf_op jit(solution)/shard_map/pallas_call | solution.py:354

commit v3 on v2

--- a/solution.py
+++ b/solution.py
@@ -34,7 +34,7 @@
     outb = rest[PARTS:2 * PARTS]
     fin = rest[2 * PARTS:3 * PARTS]
     (rate_sem, mask_sem, ring_send, ring_recv, core_send, core_recv,
-     line_send, line_recv, all_send, all_recv) = rest[3 * PARTS:]
+     line_send, line_recv, lead_send, lead_recv, all_send, all_recv) = rest[3 * PARTS:]
 
     count = groups * columns
     line, inner = line_split(columns)
@@ -139,9 +139,21 @@
             device_id=mate, device_id_type=MESH,
         )
 
+    def lead_copy(p, way, src):
+        slot = gath[p].at[pl.ds(src * TABLES + c, 1)]
+        return pltpu.make_async_remote_copy(
+            src_ref=slot, dst_ref=slot,
+            send_sem=lead_send.at[p, way], recv_sem=lead_recv.at[p, way],
+            device_id=up if way == 0 else down, device_id_type=MESH,
+        )
+
+    def line_slot(p, k, src):
+        if k == 0:
+            return gath[p].at[pl.ds(src * TABLES + (TABLES - 1 - c), 1)]
+        return gath[p].at[pl.ds(src * TABLES, TABLES)]
+
     def line_copy(p, k, way):
-        src = z - k if way == 0 else z + k
-        slot = gath[p].at[pl.ds(src * TABLES, TABLES)]
+        slot = line_slot(p, k, z - k if way == 0 else z + k)
         return pltpu.make_async_remote_copy(
             src_ref=slot, dst_ref=slot,
             send_sem=line_send.at[p, k, way], recv_sem=line_recv.at[p, k, way],
@@ -154,8 +166,7 @@
         return jnp.logical_and(z + k < line, z > 0)
 
     def line_arrival(p, k, way):
-        src = z - k - 1 if way == 0 else z + k + 1
-        slot = gath[p].at[pl.ds(src * TABLES, TABLES)]
+        slot = line_slot(p, k, z - k - 1 if way == 0 else z + k + 1)
         return pltpu.make_async_remote_copy(
             src_ref=slot, dst_ref=slot,
             send_sem=line_send.at[p, k, way], recv_sem=line_recv.at[p, k, way],
@@ -189,6 +200,10 @@
         for p in range(PARTS):
             mate_copy(p).start()
             gath[p][own] = q_out[mid - 1, c, pl.ds(p * rows, rows)]
+            for way in range(2):
+                @pl.when(line_sends(0, way))
+                def _():
+                    lead_copy(p, way, z).start()
 
     def exchange():
         step = jnp.where(c == 0, 1, count - 1)
@@ -231,6 +246,8 @@
                 for way in range(2):
                     @pl.when(line_gets(k - 1, way))
                     def _():
+                        if k == 1:
+                            lead_copy(p, way, z - 1 if way == 0 else z + 1).wait_recv()
                         line_arrival(p, k - 1, way).wait_recv()
             if k < line - 1:
                 for way in range(2):
@@ -258,6 +275,8 @@
                 for way in range(2):
                     @pl.when(line_sends(k, way))
                     def _():
+                        if k == 0:
+                            lead_copy(p, way, z).wait_send()
                         line_copy(p, k, way).wait_send()
             for i in range(len(offsets)):
                 all_copy(p, i).wait_send()
@@ -387,6 +406,7 @@
             dma((strata, TABLES, SPLIT)), dma((strata, TABLES, SPLIT)),
             dma((PARTS,)), dma((PARTS,)),
             dma((PARTS, line - 1, 2)), dma((PARTS, line - 1, 2)),
+            dma((PARTS, 2)), dma((PARTS, 2)),
             dma((PARTS, peers)), dma((PARTS, peers)),
         ]
     )

time: 86.3 us -> 85.3 us (0.988)
  Pallas kernels: 85.4 us -> 84.5 us
    pallas_call x1, Pallas kernels: 83.1 us -> 82.2 us  [body(): pl.pallas_call(functools.partial(kernel, groups, columns, strata), out_sh...]
where the time goes in v3:
time: 85.3 us; the launch traced here: 85.2 us
  Pallas kernels  84.5 us (99%)
    pallas_call x1, Pallas kernels, body(): pl.pallas_call(functools.partial(kernel, groups, columns, strata), out_sh...  82.2 us
    pallas_call x1, Pallas kernels, settle(): pl.pallas_call(copies, out_shape=shapes, in_specs=[where] * n, out_specs=...  2.38 us

profile of v3, /device:TPU:0, one launch (start us, length us, event | category | flops | bytes accessed | tf_op | source)
XLA Modules:
  0.0 85.2 jit_solution(111943072585043210)
XLA Ops:
  0.6 82.2 %shard_map.85 = (f32[1024,256]{1,0:T(8,128)}, bf16[256,256]{1,0:T(8,128)(2,1)}, bf16[256,256]{1,0:T(8,128)(2,1)}) custom-call(bf16[8,1024,512]{2,1,0:T(8,128)(2,1)} %ratings.1, s32[8,1024,512]{2,1,0:T(8,128)} %rated.1, f32[1024,256]{1,0:T(8,128)} %users_in.1, bf16[256,256]{1,0:T(8,128)(2,1)} %ahead_in.1, bf16[256,256]{1,0:T(8,128)(2,1)} %behind_in.1, ...), custom_call_target="tpu_custom_call" | custom-call | flops 6442450944 | bytes 25165824 | tf_op jit(solution)/shard_map/pallas_call | solution.py:413
  82.8 2.4 %shard_map.86 = (f32[1024,256]{1,0:T(8,128)}, bf16[256,256]{1,0:T(8,128)(2,1)}, bf16[256,256]{1,0:T(8,128)(2,1)}) custom-call(f32[1024,256]{1,0:T(8,128)} %get-tuple-element.6.refs_0_, bf16[256,256]{1,0:T(8,128)(2,1)} %get-tuple-element.7.refs_1_, bf16[256,256]{1,0:T(8,128)(2,1)} %get-tuple-element.8.refs_2_), custom_call_target="tpu_custom_call" | custom-call | tf_op jit(solution)/shard_map/pallas_call | solution.py:373

commit v4 on v3

--- a/solution.py
+++ b/solution.py
@@ -196,6 +196,26 @@
             device_id=peer(*offsets[i]), device_id_type=MESH,
         )
 
+    origin = []
+    for t in range(TABLES):
+        found = jnp.int32(0)
+        for src in range(count):
+            sg, sb = divmod(src, columns)
+            shifted = (src + (1 if t == 0 else count - 1)) % count
+            found = jnp.where(
+                owners[t, shifted] == me, (sg // TABLES) * inner + sb % inner, found
+            )
+        origin.append(t * chips + found)
+
+    def collect(i_piece):
+        for p in range(PARTS):
+            if p * SPLIT // PARTS != i_piece:
+                continue
+            for i in range(len(offsets)):
+                all_arrival(p, i).wait_recv()
+            for t in range(TABLES):
+                q_in[mid, t, pl.ds(p * rows, rows)] = fin[p][origin[t]]
+
     def exchange_start():
         for p in range(PARTS):
             mate_copy(p).start()
@@ -222,17 +242,6 @@
 
         picks = [pick(peer(*o)) for o in offsets]
         self_pick = pick((g, b))
-        origin = []
-        for t in range(TABLES):
-            found = jnp.int32(0)
-            for src in range(count):
-                sg, sb = divmod(src, columns)
-                shifted = (src + (1 if t == 0 else count - 1)) % count
-                found = jnp.where(
-                    owners[t, shifted] == me, (sg // TABLES) * inner + sb % inner, found
-                )
-            origin.append(t * chips + found)
-
         def advance(p, k):
             if k == 0:
                 arrived = pltpu.make_async_remote_copy(
@@ -264,11 +273,7 @@
             for p in range(PARTS):
                 if 0 <= wave - p < line:
                     advance(p, wave - p)
-        for p in range(PARTS):
-            for i in range(len(offsets)):
-                all_arrival(p, i).wait_recv()
-            for t in range(TABLES):
-                q_in[mid, t, pl.ds(p * rows, rows)] = fin[p][origin[t]]
+    def exchange_drain():
         for p in range(PARTS):
             mate_copy(p).wait_send()
             for k in range(line - 1):
@@ -295,6 +300,11 @@
             @pl.when(jnp.logical_and(s > 0, s != mid))
             def _():
                 ring_arrival(s, t, i).wait_recv()
+
+            if t == 0:
+                @pl.when(s == mid)
+                def _():
+                    collect(i)
 
             span = slice(i * piece, (i + 1) * piece)
             part = slice(t * half + i * piece, t * half + (i + 1) * piece)
@@ -359,6 +369,7 @@
         return carry
 
     lax.fori_loop(0, strata - 1, drain, 0)
+    exchange_drain()
 
 
 def settle(arrays):

time: 85.3 us -> 84.6 us (level)
  no operation moved by 1% of the time
where the time goes in v4:
time: 84.6 us; the launch traced here: 84.4 us
  Pallas kernels  83.8 us (99%)
    pallas_call x1, Pallas kernels, body(): pl.pallas_call(functools.partial(kernel, groups, columns, strata), out_sh...  81.4 us
    pallas_call x1, Pallas kernels, settle(): pl.pallas_call(copies, out_shape=shapes, in_specs=[where] * n, out_specs=...  2.38 us

profile of v4, /device:TPU:0, one launch (start us, length us, event | category | flops | bytes accessed | tf_op | source)
XLA Modules:
  0.0 84.4 jit_solution(7812822253773943100)
XLA Ops:
  0.6 81.4 %shard_map.85 = (f32[1024,256]{1,0:T(8,128)}, bf16[256,256]{1,0:T(8,128)(2,1)}, bf16[256,256]{1,0:T(8,128)(2,1)}) custom-call(bf16[8,1024,512]{2,1,0:T(8,128)(2,1)} %ratings.1, s32[8,1024,512]{2,1,0:T(8,128)} %rated.1, f32[1024,256]{1,0:T(8,128)} %users_in.1, bf16[256,256]{1,0:T(8,128)(2,1)} %ahead_in.1, bf16[256,256]{1,0:T(8,128)(2,1)} %behind_in.1, ...), custom_call_target="tpu_custom_call" | custom-call | flops 6442450944 | bytes 25165824 | tf_op jit(solution)/shard_map/pallas_call | solution.py:424
  82.0 2.4 %shard_map.86 = (f32[1024,256]{1,0:T(8,128)}, bf16[256,256]{1,0:T(8,128)(2,1)}, bf16[256,256]{1,0:T(8,128)(2,1)}) custom-call(f32[1024,256]{1,0:T(8,128)} %get-tuple-element.6.refs_0_, bf16[256,256]{1,0:T(8,128)(2,1)} %get-tuple-element.7.refs_1_, bf16[256,256]{1,0:T(8,128)(2,1)} %get-tuple-element.8.refs_2_), custom_call_target="tpu_custom_call" | custom-call | tf_op jit(solution)/shard_map/pallas_call | solution.py:384
